TPU v7x, 256 devices: a whole 4x4x8 slice. The times are simulated.
256 devices in a mesh: dp: 16 (over z, core), comp: 16 (over y, x).
Axes of the slice: x: 4, y: 4, z: 8, core: 2. Of those that a mesh axis runs over, the one named last changes fastest.
Arguments:
- points: bfloat16 [524288, 768], P(('dp', 'comp')), may hold values from -6 to 6
- candidates: int32 [4096, 4], P(('dp', 'comp')), may hold values from 0 to 511, as said below
- means: bfloat16 [65536, 768], P(('dp', 'comp')), may hold values from -0.59765625 to 0.59765625
- inv_var: bfloat16 [65536, 768], P(('dp', 'comp')), may hold values from 0.5 to 1.5
- log_weight: bfloat16 [65536], P(('dp', 'comp')), may hold values from -12 to -9
Outputs:
- counts: float32 [65536], P(('dp', 'comp'))
- first_moment: float32 [65536, 768], P(('dp', 'comp'))
- second_moment: float32 [65536, 768], P(('dp', 'comp'))
- loglik: float32 [524288], P(('dp', 'comp'))
Inputs may be any that keep to these rules, and one draw needn't show every extreme that they name: `candidates`: each row block names 4 different component blocks; all blocks b named by the row blocks of device index i along dp+comp satisfy (b // 2) % 16 == i % 16, that is, one owner group serves each device's rows.
All inputs are finite; a program needn't handle non-finite values.
Results may differ from a plain program's by a relative error of at most 0.028.
Values may be sent and summed in bfloat16 or wider, within the bound.
A program may use at most 128 MiB of HBM per device.

v0:
```python
import math
import jax
import jax.numpy as jnp
from jax import lax
from jax.sharding import PartitionSpec as P

CB = 128
RB = 128
CANDS = 4


def component_consts(mean_values, inv_values, log_values):
    feature_count = mean_values.shape[1]
    mean_f = mean_values.astype(jnp.float32)
    inv_f = inv_values.astype(jnp.float32)
    return (
        log_values.astype(jnp.float32)
        + 0.5 * jnp.sum(jnp.log(inv_f), axis=1)
        - 0.5 * jnp.sum(inv_f * mean_f * mean_f, axis=1)
        - 0.5 * feature_count * math.log(2.0 * math.pi)
    )


def block_terms(row_block, selector, scaled_flat, inverse_flat, constants):
    group_rows, slot_count, block_total = selector.shape
    feature_count = row_block.shape[2]
    row_f = row_block.astype(jnp.float32)
    squares = (row_f * row_f).astype(jnp.bfloat16)
    pick = selector.reshape(group_rows * slot_count, block_total)
    pick_bf = pick.astype(jnp.bfloat16)
    chosen_scaled = jnp.dot(pick_bf, scaled_flat, preferred_element_type=jnp.float32).astype(
        jnp.bfloat16
    )
    chosen_inverse = jnp.dot(pick_bf, inverse_flat, preferred_element_type=jnp.float32).astype(
        jnp.bfloat16
    )
    chosen_scaled = chosen_scaled.reshape(group_rows, slot_count, CB, feature_count)
    chosen_inverse = chosen_inverse.reshape(group_rows, slot_count, CB, feature_count)
    chosen_consts = jnp.dot(pick, constants, precision=lax.Precision.HIGHEST).reshape(
        group_rows, slot_count, CB
    )
    linear = jnp.einsum(
        "grd,gskd->grsk", row_block, chosen_scaled, preferred_element_type=jnp.float32
    )
    quadratic = jnp.einsum(
        "grd,gskd->grsk", squares, chosen_inverse, preferred_element_type=jnp.float32
    )
    densities = chosen_consts[:, None] + linear - 0.5 * quadratic
    row_peak = jnp.max(densities, axis=(2, 3))
    normalizer = row_peak + jnp.log(
        jnp.sum(jnp.exp(densities - row_peak[:, :, None, None]), axis=(2, 3))
    )
    responsibility = jnp.exp(densities - normalizer[:, :, None, None]).astype(jnp.bfloat16)
    counts = jnp.sum(responsibility.astype(jnp.float32), axis=1)
    first_moment = jnp.einsum(
        "grsk,grd->gskd", responsibility, row_block, preferred_element_type=jnp.float32
    )
    second_moment = jnp.einsum(
        "grsk,grd->gskd", responsibility, squares, preferred_element_type=jnp.float32
    )
    return (normalizer, counts, first_moment, second_moment)


def on_device(points, candidates, means, inv_var, log_weight):
    feature_count = points.shape[1]
    owner_count = lax.axis_size("comp")
    held_blocks = means.shape[0] // CB
    all_means, all_inverse, all_logs = (
        lax.all_gather(means, "dp", axis=0, tiled=True),
        lax.all_gather(inv_var, "dp", axis=0, tiled=True),
        lax.all_gather(log_weight, "dp", axis=0, tiled=True),
    )
    all_scaled = (all_inverse.astype(jnp.float32) * all_means.astype(jnp.float32)).astype(
        jnp.bfloat16
    )
    all_consts = component_consts(all_means, all_inverse, all_logs)
    group_blocks = all_scaled.shape[0] // CB
    scaled_flat = all_scaled.reshape(group_blocks, CB * feature_count)
    inverse_flat = all_inverse.reshape(group_blocks, CB * feature_count)
    constants = all_consts.reshape(group_blocks, CB)
    local_ids = candidates // (owner_count * held_blocks) * held_blocks + candidates % held_blocks
    block_count = candidates.shape[0]
    row_groups = points.reshape(block_count // 4, 4, RB, feature_count)
    id_groups = local_ids.reshape(block_count // 4, 4, CANDS)
    block_iota = jnp.arange(group_blocks, dtype=jnp.int32)

    def accumulate(running, inputs):
        row_block, chosen_ids = inputs
        selector = (chosen_ids[:, :, None] == block_iota[None, None, :]).astype(jnp.float32)
        normalizer, counts, first_part, second_part = block_terms(
            row_block, selector, scaled_flat, inverse_flat, constants
        )
        spread = selector.reshape(-1, group_blocks).T
        slot_total = spread.shape[1]
        new_counts = jnp.dot(
            spread, counts.reshape(slot_total, CB), precision=lax.Precision.HIGHEST
        )
        new_first = jnp.dot(
            spread,
            first_part.reshape(slot_total, CB * feature_count),
            precision=lax.Precision.HIGHEST,
        )
        new_second = jnp.dot(
            spread,
            second_part.reshape(slot_total, CB * feature_count),
            precision=lax.Precision.HIGHEST,
        )
        running = (running[0] + new_counts, running[1] + new_first, running[2] + new_second)
        return (running, normalizer)

    initial = (
        jnp.zeros((group_blocks, CB), jnp.float32),
        jnp.zeros((group_blocks, CB * feature_count), jnp.float32),
        jnp.zeros((group_blocks, CB * feature_count), jnp.float32),
    )
    partials, normalizers = lax.scan(accumulate, initial, (row_groups, id_groups))
    count_sum, first_sum, second_sum = (
        lax.psum_scatter(
            partials[0].astype(jnp.bfloat16), "dp", scatter_dimension=0, tiled=True
        ).astype(jnp.float32),
        lax.psum_scatter(
            partials[1].astype(jnp.bfloat16), "dp", scatter_dimension=0, tiled=True
        ).astype(jnp.float32),
        lax.psum_scatter(
            partials[2].astype(jnp.bfloat16), "dp", scatter_dimension=0, tiled=True
        ).astype(jnp.float32),
    )
    loglik = normalizers.reshape(-1) / feature_count
    return (
        count_sum.reshape(-1),
        first_sum.reshape(-1, feature_count),
        second_sum.reshape(-1, feature_count),
        loglik,
    )


def solution(mesh):
    return jax.shard_map(
        on_device,
        mesh=mesh,
        in_specs=(
            P(("dp", "comp"), None),
            P(("dp", "comp"), None),
            P(("dp", "comp"), None),
            P(("dp", "comp"), None),
            P(("dp", "comp")),
        ),
        out_specs=(
            P(("dp", "comp")),
            P(("dp", "comp"), None),
            P(("dp", "comp"), None),
            P(("dp", "comp")),
        ),
        check_vma=False,
    )
```

profile of v0, /device:TPU:2, one launch (start us, length us, event | category | flops | bytes accessed | tf_op | source)
XLA Modules:
  0.0 519.8 jit_solution(4086402239218131101)
XLA Ops:
  7.2 0.7 all-gather.4.cloned.1.call-update
  7.9 0.7 all-gather.6.cloned.1.call-update
  9.4 20.0 %all-gather = bf16[16,1,256]{2,1,0:T(2,128)(2,1)S(1)} all-gather(bf16[1,1,256]{2,1,0:T(2,128)(2,1)S(1)} %reshape.127), channel_id=1, replica_groups=mesh['dp'=16,'comp'=16] {'dp'}, dimensions={0}, use_global_device_ids=true | all-gather | bytes 8704 | tf_op jit(solution)/shard_map/all_gather | solution.py:71
  29.4 0.7 fusion.36
  30.2 28.7 %all-gather.4.cloned.1.call-done = bf16[4096,768]{1,0:T(8,128)(2,1)} async-done(((bf16[256,768]{1,0:T(8,128)(2,1)}), bf16[4096,768]{1,0:T(8,128)(2,1)}) %all-gather.4.cloned.1.call-update) | async-done | bytes 6291472 | tf_op jit(solution)/shard_map/all_gather | solution.py:70
  58.9 46.5 %all-gather.6.cloned.1.call-done = bf16[4096,768]{1,0:T(8,128)(2,1)} async-done(((bf16[256,768]{1,0:T(8,128)(2,1)}), bf16[4096,768]{1,0:T(8,128)(2,1)}) %all-gather.6.cloned.1.call-update) | async-done | bytes 6291472 | tf_op jit(solution)/shard_map/all_gather | solution.py:69
  105.4 10.6 %fusion.32 = (f32[4096]{0:T(1024)S(1)}, f32[4096]{0:T(1024)S(1)}, bf16[4096,768]{1,0:T(8,128)(2,1)}) fusion(bf16[4096,768]{1,0:T(8,128)(2,1)} %all-gather.4.cloned.1.call-done, bf16[4096,768]{1,0:T(8,128)(2,1)} %all-gather.6.cloned.1.call-done), kind=kLoop, calls=%fused_computation.46 | loop fusion | flops 22011904 | bytes 18907136 | tf_op jit(solution)/shard_map/reduce_sum | solution.py:18
  115.9 7.2 %reshape.109 = bf16[32,98304]{1,0:T(8,128)(2,1)} reshape(bf16[4096,768]{1,0:T(8,128)(2,1)} %get-tuple-element.182) | data formatting | bytes 12582912 | tf_op jit(solution)/shard_map/reshape | solution.py:78
  123.2 7.3 %reshape.110 = bf16[32,98304]{1,0:T(8,128)(2,1)} reshape(bf16[4096,768]{1,0:T(8,128)(2,1)} %all-gather.4.cloned.1.call-done) | data formatting | bytes 12582912 | tf_op jit(solution)/shard_map/reshape | solution.py:79
  130.5 203.8 %while.18 = (s32[]{:T(128)}, f32[32,128]{1,0:T(8,128)S(1)}, f32[32,98304]{1,0:T(8,128)}, f32[32,98304]{1,0:T(8,128)}, f32[4,4,128]{2,1,0:T(4,128)S(1)}, /*index=...) while((s32[]{:T(128)}, f32[32,128]{1,0:T(8,128)S(1)}, ...), condition=%wide.region_6.7_spmd.clone.clone, body=%wide.region_2.6_spmd.clone.clone.sunk | while | flops 3042191872 | bytes 255429680 | solution.py:116
  130.6 4.0 convolution_convert_fusion.4
  134.6 0.7 copy.22
  135.5 2.1 convolution_add_fusion.6
  137.7 1.0 convolution_convert_fusion.5
  138.7 0.7 copy.23
  139.4 2.1 fusion.90
  142.1 2.1 fusion.92
  144.2 6.3 %copy.24 = f32[2,8,128,768]{3,1,2,0:T(8,128)} copy(f32[2,8,128,768]{3,2,1,0:T(8,128)S(1)} %bitcast.122) | data formatting | bytes 12582912 | tf_op jit(solution)/shard_map/while
  150.5 10.6 %convolution_add_fusion.7 = f32[32,98304]{1,0:T(8,128)} fusion(f32[16,98304]{1,0:T(8,128)} %bitcast.119, f32[32,98304]{1,0:T(8,128)} %get-tuple-element.272, pred[]{:T(512)S(6)} %compare.6, s32[16]{0:T(128)S(1)} %eq.108), kind=kOutput, calls=%fused_computation.2.clone.1 | convolution fusion | flops 610271744 | bytes 31457344 | tf_op jit(solution)/shard_map/while/body/eval_jaxpr/dot_general | solution.py:98
  161.1 2.3 fusion.93
  163.4 3.6 copy.25
  167.0 8.2 %convolution_add_fusion.8 = f32[32,98304]{1,0:T(8,128)S(1)} fusion(f32[16,98304]{1,0:T(8,128)S(1)} %bitcast.120, f32[32,98304]{1,0:T(8,128)S(1)} %bitcast.126, pred[]{:T(512)S(6)} %compare.6, s32[16]{0:T(128)S(1)} %eq.108), kind=kOutput, calls=%fused_computation.1.clone.1 | convolution fusion | flops 610271744 | bytes 31457344 | tf_op jit(solution)/shard_map/while/body/eval_jaxpr/dot_general | solution.py:103
  175.3 4.5 copy-done
  180.1 4.0 convolution_convert_fusion.4
  184.1 0.7 copy.22
  185.0 2.1 convolution_add_fusion.6
  187.2 1.0 convolution_convert_fusion.5
  188.9 2.1 fusion.90
  191.6 2.1 fusion.92
  193.7 6.3 %copy.24 = f32[2,8,128,768]{3,1,2,0:T(8,128)} copy(f32[2,8,128,768]{3,2,1,0:T(8,128)S(1)} %bitcast.122) | data formatting | bytes 12582912 | tf_op jit(solution)/shard_map/while
  200.0 12.5 %convolution_add_fusion.7 = f32[32,98304]{1,0:T(8,128)} fusion(f32[16,98304]{1,0:T(8,128)} %bitcast.119, f32[32,98304]{1,0:T(8,128)} %get-tuple-element.272, pred[]{:T(512)S(6)} %compare.6, s32[16]{0:T(128)S(1)} %eq.108), kind=kOutput, calls=%fused_computation.2.clone.1 | convolution fusion | flops 610271744 | bytes 31457344 | tf_op jit(solution)/shard_map/while/body/eval_jaxpr/dot_general | solution.py:98
  212.5 2.3 fusion.93
  214.7 3.6 copy.25
  218.4 8.2 %convolution_add_fusion.8 = f32[32,98304]{1,0:T(8,128)S(1)} fusion(f32[16,98304]{1,0:T(8,128)S(1)} %bitcast.120, f32[32,98304]{1,0:T(8,128)S(1)} %bitcast.126, pred[]{:T(512)S(6)} %compare.6, s32[16]{0:T(128)S(1)} %eq.108), kind=kOutput, calls=%fused_computation.1.clone.1 | convolution fusion | flops 610271744 | bytes 31457344 | tf_op jit(solution)/shard_map/while/body/eval_jaxpr/dot_general | solution.py:103
  226.6 4.5 copy-done
  231.5 4.0 convolution_convert_fusion.4
  236.4 2.1 convolution_add_fusion.6
  238.5 1.0 convolution_convert_fusion.5
  240.3 2.1 fusion.90
  242.9 2.1 fusion.92
  245.0 6.3 %copy.24 = f32[2,8,128,768]{3,1,2,0:T(8,128)} copy(f32[2,8,128,768]{3,2,1,0:T(8,128)S(1)} %bitcast.122) | data formatting | bytes 12582912 | tf_op jit(solution)/shard_map/while
  251.3 12.5 %convolution_add_fusion.7 = f32[32,98304]{1,0:T(8,128)} fusion(f32[16,98304]{1,0:T(8,128)} %bitcast.119, f32[32,98304]{1,0:T(8,128)} %get-tuple-element.272, pred[]{:T(512)S(6)} %compare.6, s32[16]{0:T(128)S(1)} %eq.108), kind=kOutput, calls=%fused_computation.2.clone.1 | convolution fusion | flops 610271744 | bytes 31457344 | tf_op jit(solution)/shard_map/while/body/eval_jaxpr/dot_general | solution.py:98
  263.8 2.3 fusion.93
  266.1 3.6 copy.25
  269.8 8.2 %convolution_add_fusion.8 = f32[32,98304]{1,0:T(8,128)S(1)} fusion(f32[16,98304]{1,0:T(8,128)S(1)} %bitcast.120, f32[32,98304]{1,0:T(8,128)S(1)} %bitcast.126, pred[]{:T(512)S(6)} %compare.6, s32[16]{0:T(128)S(1)} %eq.108), kind=kOutput, calls=%fused_computation.1.clone.1 | convolution fusion | flops 610271744 | bytes 31457344 | tf_op jit(solution)/shard_map/while/body/eval_jaxpr/dot_general | solution.py:103
  278.0 4.5 copy-done
  282.8 4.0 convolution_convert_fusion.4
  287.7 2.1 convolution_add_fusion.6
  289.9 1.0 convolution_convert_fusion.5
  291.6 2.1 fusion.90
  294.3 2.1 fusion.92
  296.4 6.3 %copy.24 = f32[2,8,128,768]{3,1,2,0:T(8,128)} copy(f32[2,8,128,768]{3,2,1,0:T(8,128)S(1)} %bitcast.122) | data formatting | bytes 12582912 | tf_op jit(solution)/shard_map/while
  302.7 12.5 %convolution_add_fusion.7 = f32[32,98304]{1,0:T(8,128)} fusion(f32[16,98304]{1,0:T(8,128)} %bitcast.119, f32[32,98304]{1,0:T(8,128)} %get-tuple-element.272, pred[]{:T(512)S(6)} %compare.6, s32[16]{0:T(128)S(1)} %eq.108), kind=kOutput, calls=%fused_computation.2.clone.1 | convolution fusion | flops 610271744 | bytes 31457344 | tf_op jit(solution)/shard_map/while/body/eval_jaxpr/dot_general | solution.py:98
  315.2 2.3 fusion.93
  317.4 3.6 copy.25
  321.1 8.2 %convolution_add_fusion.8 = f32[32,98304]{1,0:T(8,128)S(1)} fusion(f32[16,98304]{1,0:T(8,128)S(1)} %bitcast.120, f32[32,98304]{1,0:T(8,128)S(1)} %bitcast.126, pred[]{:T(512)S(6)} %compare.6, s32[16]{0:T(128)S(1)} %eq.108), kind=kOutput, calls=%fused_computation.1.clone.1 | convolution fusion | flops 610271744 | bytes 31457344 | tf_op jit(solution)/shard_map/while/body/eval_jaxpr/dot_general | solution.py:103
  329.3 4.5 copy-done
  334.3 7.9 %convert_element_type.56 = bf16[32,98304]{1,0:T(8,128)(2,1)} convert(f32[32,98304]{1,0:T(8,128)} %get-tuple-element.68) | non-fusion elementwise | flops 3145728 | bytes 18874368 | tf_op jit(solution)/shard_map/convert_element_type | solution.py:122
  342.2 7.9 %convert_element_type.57 = bf16[32,98304]{1,0:T(8,128)(2,1)} convert(f32[32,98304]{1,0:T(8,128)} %get-tuple-element.69) | non-fusion elementwise | flops 3145728 | bytes 18874368 | tf_op jit(solution)/shard_map/convert_element_type | solution.py:125
  352.0 26.5 %all-reduce = bf16[32,128]{1,0:T(8,128)(2,1)S(1)} all-reduce(bf16[32,128]{1,0:T(8,128)(2,1)S(1)} %convert_element_type.55), channel_id=2, replica_groups=mesh['dp'=16,'comp'=16] {'dp'}, use_global_device_ids=true, to_apply=%region_7.8.clone | all-reduce | flops 4096 | bytes 16384
  379.6 128.0 %all-reduce.6.cloned.1.call-done = (bf16[32,98304]{1,0:T(8,128)(2,1)}, bf16[32,98304]{1,0:T(8,128)(2,1)}) async-done(((bf16[32,98304]{1,0:T(8,128)(2,1)}, bf16[32,98304]{1,0:T(8,128)(2,1)}), (bf16[32,98304]{1,0:T(8,128)(2,1)}, bf16[32,98304]{1,0:T(8,128)(2,1)})) %all-reduce.6.cloned.1.call-update) | async-done | bytes 12582928
  507.6 2.5 dynamic-slice_convert_fusion
  510.1 1.6 reshape.124
  511.7 1.6 reshape.126
  (107 shorter events, 11.3 us)
Async XLA Ops:
  7.2 51.7 %all-gather.4.cloned.1.call-start = ((), (), s32[]{:S(2)}) async-start(), calls=%async_computation | async-start | bytes 6684672 | tf_op jit(solution)/shard_map/all_gather | solution.py:70
  7.9 97.5 %all-gather.6.cloned.1.call-start = ((), (), s32[]{:S(2)}) async-start(), calls=%async_computation.1 | async-start | bytes 6684672 | tf_op jit(solution)/shard_map/all_gather | solution.py:69
  8.6 499.0 %all-reduce.6.cloned.1.call-start = ((), (), s32[]{:S(2)}) async-start(), calls=%async_computation.2 | async-start | bytes 25165824
  130.6 7.0 %slice-start.3 = ((s8[6291456]{0:T(1024)(128)(4,1)}), s8[4194304]{0:T(1024)(128)(4,1)S(1)}, s32[]{:S(2)}) async-start(s8[6291456]{0:T(1024)(128)(4,1)} %bitcast.129), calls=%async_computation.6 | async-start | bytes 8388608 | tf_op jit(solution)/shard_map/while
  134.6 3.1 slice-start.4
  150.5 16.6 %slice-start = ((s8[12582912]{0:T(1024)(128)(4,1)}), s8[4194304]{0:T(1024)(128)(4,1)S(1)}, s32[]{:S(2)}) async-start(s8[12582912]{0:T(1024)(128)(4,1)} %bitcast.125), calls=%async_computation.3 | async-start | bytes 8388608 | tf_op jit(solution)/shard_map/while
  150.5 16.6 %slice-start.1 = ((s8[12582912]{0:T(1024)(128)(4,1)}), s8[4194304]{0:T(1024)(128)(4,1)S(1)}, s32[]{:S(2)}) async-start(s8[12582912]{0:T(1024)(128)(4,1)} %bitcast.125), calls=%async_computation.4 | async-start | bytes 8388608 | tf_op jit(solution)/shard_map/while
  161.1 5.9 %slice-start.2 = ((s8[12582912]{0:T(1024)(128)(4,1)}), s8[4194304]{0:T(1024)(128)(4,1)S(1)}, s32[]{:S(2)}) async-start(s8[12582912]{0:T(1024)(128)(4,1)} %bitcast.125), calls=%async_computation.5 | async-start | bytes 8388608 | tf_op jit(solution)/shard_map/while
  175.2 4.5 copy-start
  180.1 7.0 %slice-start.3 = ((s8[6291456]{0:T(1024)(128)(4,1)}), s8[4194304]{0:T(1024)(128)(4,1)S(1)}, s32[]{:S(2)}) async-start(s8[6291456]{0:T(1024)(128)(4,1)} %bitcast.129), calls=%async_computation.6 | async-start | bytes 8388608 | tf_op jit(solution)/shard_map/while
  184.1 3.1 slice-start.4
  200.0 18.4 %slice-start = ((s8[12582912]{0:T(1024)(128)(4,1)}), s8[4194304]{0:T(1024)(128)(4,1)S(1)}, s32[]{:S(2)}) async-start(s8[12582912]{0:T(1024)(128)(4,1)} %bitcast.125), calls=%async_computation.3 | async-start | bytes 8388608 | tf_op jit(solution)/shard_map/while
  200.0 18.4 %slice-start.1 = ((s8[12582912]{0:T(1024)(128)(4,1)}), s8[4194304]{0:T(1024)(128)(4,1)S(1)}, s32[]{:S(2)}) async-start(s8[12582912]{0:T(1024)(128)(4,1)} %bitcast.125), calls=%async_computation.4 | async-start | bytes 8388608 | tf_op jit(solution)/shard_map/while
  212.5 5.9 %slice-start.2 = ((s8[12582912]{0:T(1024)(128)(4,1)}), s8[4194304]{0:T(1024)(128)(4,1)S(1)}, s32[]{:S(2)}) async-start(s8[12582912]{0:T(1024)(128)(4,1)} %bitcast.125), calls=%async_computation.5 | async-start | bytes 8388608 | tf_op jit(solution)/shard_map/while
  226.6 4.5 copy-start
  231.5 7.0 %slice-start.3 = ((s8[6291456]{0:T(1024)(128)(4,1)}), s8[4194304]{0:T(1024)(128)(4,1)S(1)}, s32[]{:S(2)}) async-start(s8[6291456]{0:T(1024)(128)(4,1)} %bitcast.129), calls=%async_computation.6 | async-start | bytes 8388608 | tf_op jit(solution)/shard_map/while
  235.5 3.1 slice-start.4
  251.3 18.4 %slice-start = ((s8[12582912]{0:T(1024)(128)(4,1)}), s8[4194304]{0:T(1024)(128)(4,1)S(1)}, s32[]{:S(2)}) async-start(s8[12582912]{0:T(1024)(128)(4,1)} %bitcast.125), calls=%async_computation.3 | async-start | bytes 8388608 | tf_op jit(solution)/shard_map/while
  251.3 18.4 %slice-start.1 = ((s8[12582912]{0:T(1024)(128)(4,1)}), s8[4194304]{0:T(1024)(128)(4,1)S(1)}, s32[]{:S(2)}) async-start(s8[12582912]{0:T(1024)(128)(4,1)} %bitcast.125), calls=%async_computation.4 | async-start | bytes 8388608 | tf_op jit(solution)/shard_map/while
  263.8 5.9 %slice-start.2 = ((s8[12582912]{0:T(1024)(128)(4,1)}), s8[4194304]{0:T(1024)(128)(4,1)S(1)}, s32[]{:S(2)}) async-start(s8[12582912]{0:T(1024)(128)(4,1)} %bitcast.125), calls=%async_computation.5 | async-start | bytes 8388608 | tf_op jit(solution)/shard_map/while
  278.0 4.5 copy-start
  282.8 7.0 %slice-start.3 = ((s8[6291456]{0:T(1024)(128)(4,1)}), s8[4194304]{0:T(1024)(128)(4,1)S(1)}, s32[]{:S(2)}) async-start(s8[6291456]{0:T(1024)(128)(4,1)} %bitcast.129), calls=%async_computation.6 | async-start | bytes 8388608 | tf_op jit(solution)/shard_map/while
  286.8 3.1 slice-start.4
  302.7 18.4 %slice-start = ((s8[12582912]{0:T(1024)(128)(4,1)}), s8[4194304]{0:T(1024)(128)(4,1)S(1)}, s32[]{:S(2)}) async-start(s8[12582912]{0:T(1024)(128)(4,1)} %bitcast.125), calls=%async_computation.3 | async-start | bytes 8388608 | tf_op jit(solution)/shard_map/while
  302.7 18.4 %slice-start.1 = ((s8[12582912]{0:T(1024)(128)(4,1)}), s8[4194304]{0:T(1024)(128)(4,1)S(1)}, s32[]{:S(2)}) async-start(s8[12582912]{0:T(1024)(128)(4,1)} %bitcast.125), calls=%async_computation.4 | async-start | bytes 8388608 | tf_op jit(solution)/shard_map/while
  315.2 5.9 %slice-start.2 = ((s8[12582912]{0:T(1024)(128)(4,1)}), s8[4194304]{0:T(1024)(128)(4,1)S(1)}, s32[]{:S(2)}) async-start(s8[12582912]{0:T(1024)(128)(4,1)} %bitcast.125), calls=%async_computation.5 | async-start | bytes 8388608 | tf_op jit(solution)/shard_map/while
  329.3 4.5 copy-start
  350.0 0.7 copy-start.1
Sparse Core Ops, SparseCore 0:
  9.8 48.9 all-gather.3
  60.7 44.6 all-gather.5
  350.2 157.3 all-reduce.5
where the time goes:
time: 521 us; the launch traced here: 520 us
  waiting for transfers between devices  205 us (39%)
  matrix products  137 us (26%)
  local copies, waits for them, and re-layouts  83.2 us (16%)
  blocking collectives  46.4 us (9%)
  other arithmetic  32.9 us (6%)
  between operations  14.5 us (3%)
    unnamed x4, waiting for transfers between devices  129 us
    while x64, local copies, waits for them, and re-layouts  63.1 us
    dot_general x4, matrix products, accumulate(): jnp.dot(spread, first_part.reshape(slot_total, CB * feature_count), preci...  48.1 us
    all_gather x1, waiting for transfers between devices, on_device(): lax.all_gather(means, 'dp', axis=0, tiled=True)  46.5 us
    dot_general x4, matrix products, accumulate(): jnp.dot(spread, second_part.reshape(slot_total, CB * feature_count), prec...  32.8 us
    all_gather x1, waiting for transfers between devices, on_device(): lax.all_gather(inv_var, 'dp', axis=0, tiled=True)  28.7 us
    unnamed x1, blocking collectives  26.5 us
    all_gather x1, blocking collectives, on_device(): lax.all_gather(log_weight, 'dp', axis=0, tiled=True)  20 us
  transfers between devices with their start and end apart: 3, of which 3 were waited for; matrix products, arithmetic and copies ran while one was open for 1% of the time, Pallas kernels for 0%

commit v1 on v0

--- a/solution.py
+++ b/solution.py
@@ -65,9 +65,16 @@
     feature_count = points.shape[1]
     owner_count = lax.axis_size("comp")
     held_blocks = means.shape[0] // CB
+
+    def _unite_vector(x_local, which_dim):
+        s_next = lax.all_to_all(
+            jnp.stack(tuple((x_local for _ in range(lax.axis_size("dp"))))), "dp", 0, 0
+        )
+        return jnp.concatenate(s_next, which_dim)
+
     all_means, all_inverse, all_logs = (
         lax.all_gather(means, "dp", axis=0, tiled=True),
-        lax.all_gather(inv_var, "dp", axis=0, tiled=True),
+        _unite_vector(inv_var, 0),
         lax.all_gather(log_weight, "dp", axis=0, tiled=True),
     )
     all_scaled = (all_inverse.astype(jnp.float32) * all_means.astype(jnp.float32)).astype(

time: 521 us -> 643 us (1.23)
  blocking collectives: 46.4 us -> 203 us
  waiting for transfers between devices: 205 us -> 132 us
  loops' own time: 0.92 us -> 18.2 us
  starting transfers between devices: 0.11 us -> 8.82 us
    all_gather x1, blocking collectives: 20 us -> 178 us  [on_device(): lax.all_gather(log_weight, 'dp', axis=0, tiled=True)]
    all_gather x1, waiting for transfers between devices: 46.5 us -> 0.02 us  [on_device(): lax.all_gather(means, 'dp', axis=0, tiled=True)]
    all_gather x1 -> x0, waiting for transfers between devices: 28.7 us -> none  [on_device(): lax.all_gather(inv_var, 'dp', axis=0, tiled=True)]
    another operation x1, loops' own time: 0.92 us -> 18.2 us  [on_device(): lax.scan(accumulate, initial, (row_groups, id_groups))]
    another operation x0 -> x2, local copies, waits for them, and re-layouts: none -> 11.6 us  [the longest x1 7.31 us: on_device(): inverse_flat = all_inverse.reshape(group_blocks, CB * feature_count)]
    convert_element_type x0 -> x1, other arithmetic: none -> 9.57 us  [on_device(): (all_inverse.astype(jnp.float32) * all_means.astype(jnp.float32)).astype(...]
    all_to_all x0 -> x1, starting transfers between devices: none -> 8.75 us  [_unite_vector(): lax.all_to_all(jnp.stack(tuple((x_local for _ in range(lax.axis_size('dp'...]
    reshape x1 -> x0, local copies, waits for them, and re-layouts: 7.31 us -> none  [on_device(): inverse_flat = all_inverse.reshape(group_blocks, CB * feature_count)]
  transfers between devices with their start and end apart: 3 -> 3, of which waited for: 3 -> 1; matrix products, arithmetic and copies ran while one was open for 1% -> 1% of each run, Pallas kernels for 0% -> 0%
where the time goes in v1:
time: 643 us; the launch traced here: 637 us
  blocking collectives  203 us (32%)
  matrix products  137 us (21%)
  waiting for transfers between devices  132 us (21%)
  local copies, waits for them, and re-layouts  86.8 us (13%)
  other arithmetic  35.8 us (6%)
  loops' own time  18.2 us (3%)
  between operations  15.2 us (2%)
  starting transfers between devices  8.82 us (1%)
    all_gather x1, blocking collectives, on_device(): lax.all_gather(log_weight, 'dp', axis=0, tiled=True)  178 us
    unnamed x3, waiting for transfers between devices  132 us
    while x64, local copies, waits for them, and re-layouts  63.1 us
    dot_general x4, matrix products, accumulate(): jnp.dot(spread, first_part.reshape(slot_total, CB * feature_count), preci...  48.1 us
    dot_general x4, matrix products, accumulate(): jnp.dot(spread, second_part.reshape(slot_total, CB * feature_count), prec...  32.8 us
    unnamed x1, blocking collectives  24.9 us
    another operation x1, loops' own time, on_device(): lax.scan(accumulate, initial, (row_groups, id_groups))  18.2 us
    dot_general x4, matrix products, block_terms(): jnp.dot(pick_bf, scaled_flat, preferred_element_type=jnp.float32)  15.9 us
  transfers between devices with their start and end apart: 3, of which 1 were waited for; matrix products, arithmetic and copies ran while one was open for 1% of the time, Pallas kernels for 0%

profile of v1, /device:TPU:2, one launch (start us, length us, event | category | flops | bytes accessed | tf_op | source)
XLA Modules:
  0.0 637.1 jit_solution(17060317489978299087)
XLA Ops:
  7.2 4.3 stack.2
  11.5 8.7 %all-to-all-start = ((bf16[16,256,768]{2,1,0:T(8,128)(2,1)}), bf16[16,256,768]{2,1,0:T(8,128)(2,1)}, u32[]{:S(2)}, u32[]{:S(2)}) async-start(bf16[16,256,768]{2,1,0:T(8,128)(2,1)} %stack.2), calls=%async_computation | async-start | bytes 12582912 | tf_op jit(solution)/shard_map/all_to_all | solution.py:70
  20.3 0.7 all-gather.3.cloned.1.call-update
  21.1 178.1 %all-gather = bf16[16,1,256]{2,1,0:T(2,128)(2,1)S(1)} all-gather(bf16[1,1,256]{2,1,0:T(2,128)(2,1)S(1)} %reshape.132), channel_id=1, replica_groups=mesh['dp'=16,'comp'=16] {'dp'}, dimensions={0}, use_global_device_ids=true | all-gather | bytes 8704 | tf_op jit(solution)/shard_map/all_gather | solution.py:78
  199.3 4.6 log_reduce_fusion
  204.0 9.6 %fusion.32 = (bf16[4096,768]{1,0:T(8,128)(2,1)}, f32[4096]{0:T(1024)S(1)}) fusion(bf16[4096,768]{1,0:T(8,128)(2,1)} %all-gather.3.cloned.1.call-done, bf16[16,256,768]{2,1,0:T(8,128)(2,1)} %all-to-all-done), kind=kLoop, calls=%fused_computation.46 | loop fusion | flops 18870272 | bytes 18890752 | tf_op jit(solution)/shard_map/convert_element_type | solution.py:80
  213.6 7.3 %reshape.114 = bf16[32,98304]{1,0:T(8,128)(2,1)} reshape(bf16[4096,768]{1,0:T(8,128)(2,1)} %get-tuple-element.180) | data formatting | bytes 12582912 | tf_op jit(solution)/shard_map/reshape | solution.py:85
  220.9 7.3 %reshape_reshape.3 = bf16[32,98304]{1,0:T(8,128)(2,1)} reshape(bf16[16,256,768]{2,1,0:T(8,128)(2,1)} %all-to-all-done) | data formatting | bytes 12582912 | tf_op jit(solution)/shard_map/reshape;reshape | solution.py:86
  228.2 221.0 %while.18 = (s32[]{:T(128)}, f32[32,128]{1,0:T(8,128)S(1)}, f32[32,98304]{1,0:T(8,128)}, f32[32,98304]{1,0:T(8,128)}, f32[4,4,128]{2,1,0:T(4,128)S(1)}, /*index=...) while((s32[]{:T(128)}, f32[32,128]{1,0:T(8,128)S(1)}, ...), condition=%wide.region_6.7_spmd.clone.clone, body=%wide.region_2.6_spmd.clone.clone.sunk | while | flops 3042191872 | bytes 255429680 | solution.py:123
  245.6 4.0 convolution_convert_fusion.4
  249.6 0.7 copy.23
  250.5 2.1 convolution_add_fusion.6
  252.6 1.0 convolution_convert_fusion.5
  253.7 0.7 copy.24
  254.3 2.1 fusion.89
  257.0 2.1 fusion.91
  259.1 6.3 copy.25
  265.4 10.7 %convolution_add_fusion.7 = f32[32,98304]{1,0:T(8,128)} fusion(f32[16,98304]{1,0:T(8,128)} %bitcast.128, f32[32,98304]{1,0:T(8,128)} %get-tuple-element.271, pred[]{:T(512)S(6)} %compare.6, s32[16]{0:T(128)S(1)} %eq.108), kind=kOutput, calls=%fused_computation.2.clone.1 | convolution fusion | flops 610271744 | bytes 31457344 | tf_op jit(solution)/shard_map/while/body/eval_jaxpr/dot_general | solution.py:105
  276.1 2.3 fusion.92
  278.3 3.6 copy.26
  282.0 8.2 %convolution_add_fusion.8 = f32[32,98304]{1,0:T(8,128)S(1)} fusion(f32[16,98304]{1,0:T(8,128)S(1)} %bitcast.129, f32[32,98304]{1,0:T(8,128)S(1)} %bitcast.135, pred[]{:T(512)S(6)} %compare.6, s32[16]{0:T(128)S(1)} %eq.108), kind=kOutput, calls=%fused_computation.1.clone.1 | convolution fusion | flops 610271744 | bytes 31457344 | tf_op jit(solution)/shard_map/while/body/eval_jaxpr/dot_general | solution.py:110
  290.2 4.5 copy-done
  295.1 4.0 convolution_convert_fusion.4
  299.1 0.7 copy.23
  300.0 2.1 convolution_add_fusion.6
  302.1 1.0 convolution_convert_fusion.5
  303.9 2.1 fusion.89
  306.6 2.1 fusion.91
  308.6 6.3 copy.25
  314.9 12.5 %convolution_add_fusion.7 = f32[32,98304]{1,0:T(8,128)} fusion(f32[16,98304]{1,0:T(8,128)} %bitcast.128, f32[32,98304]{1,0:T(8,128)} %get-tuple-element.271, pred[]{:T(512)S(6)} %compare.6, s32[16]{0:T(128)S(1)} %eq.108), kind=kOutput, calls=%fused_computation.2.clone.1 | convolution fusion | flops 610271744 | bytes 31457344 | tf_op jit(solution)/shard_map/while/body/eval_jaxpr/dot_general | solution.py:105
  327.4 2.3 fusion.92
  329.7 3.6 copy.26
  333.4 8.2 %convolution_add_fusion.8 = f32[32,98304]{1,0:T(8,128)S(1)} fusion(f32[16,98304]{1,0:T(8,128)S(1)} %bitcast.129, f32[32,98304]{1,0:T(8,128)S(1)} %bitcast.135, pred[]{:T(512)S(6)} %compare.6, s32[16]{0:T(128)S(1)} %eq.108), kind=kOutput, calls=%fused_computation.1.clone.1 | convolution fusion | flops 610271744 | bytes 31457344 | tf_op jit(solution)/shard_map/while/body/eval_jaxpr/dot_general | solution.py:110
  341.6 4.5 copy-done
  346.4 4.0 convolution_convert_fusion.4
  350.4 0.7 copy.23
  351.3 2.1 convolution_add_fusion.6
  353.5 1.0 convolution_convert_fusion.5
  355.2 2.1 fusion.89
  357.9 2.1 fusion.91
  360.0 6.3 copy.25
  366.3 12.5 %convolution_add_fusion.7 = f32[32,98304]{1,0:T(8,128)} fusion(f32[16,98304]{1,0:T(8,128)} %bitcast.128, f32[32,98304]{1,0:T(8,128)} %get-tuple-element.271, pred[]{:T(512)S(6)} %compare.6, s32[16]{0:T(128)S(1)} %eq.108), kind=kOutput, calls=%fused_computation.2.clone.1 | convolution fusion | flops 610271744 | bytes 31457344 | tf_op jit(solution)/shard_map/while/body/eval_jaxpr/dot_general | solution.py:105
  378.8 2.3 fusion.92
  381.0 3.6 copy.26
  384.7 8.2 %convolution_add_fusion.8 = f32[32,98304]{1,0:T(8,128)S(1)} fusion(f32[16,98304]{1,0:T(8,128)S(1)} %bitcast.129, f32[32,98304]{1,0:T(8,128)S(1)} %bitcast.135, pred[]{:T(512)S(6)} %compare.6, s32[16]{0:T(128)S(1)} %eq.108), kind=kOutput, calls=%fused_computation.1.clone.1 | convolution fusion | flops 610271744 | bytes 31457344 | tf_op jit(solution)/shard_map/while/body/eval_jaxpr/dot_general | solution.py:110
  392.9 4.5 copy-done
  397.8 4.0 convolution_convert_fusion.4
  402.7 2.1 convolution_add_fusion.6
  404.8 1.0 convolution_convert_fusion.5
  406.6 2.1 fusion.89
  409.3 2.1 fusion.91
  411.4 6.3 copy.25
  417.6 12.5 %convolution_add_fusion.7 = f32[32,98304]{1,0:T(8,128)} fusion(f32[16,98304]{1,0:T(8,128)} %bitcast.128, f32[32,98304]{1,0:T(8,128)} %get-tuple-element.271, pred[]{:T(512)S(6)} %compare.6, s32[16]{0:T(128)S(1)} %eq.108), kind=kOutput, calls=%fused_computation.2.clone.1 | convolution fusion | flops 610271744 | bytes 31457344 | tf_op jit(solution)/shard_map/while/body/eval_jaxpr/dot_general | solution.py:105
  430.1 2.3 fusion.92
  432.4 3.6 copy.26
  436.1 8.2 %convolution_add_fusion.8 = f32[32,98304]{1,0:T(8,128)S(1)} fusion(f32[16,98304]{1,0:T(8,128)S(1)} %bitcast.129, f32[32,98304]{1,0:T(8,128)S(1)} %bitcast.135, pred[]{:T(512)S(6)} %compare.6, s32[16]{0:T(128)S(1)} %eq.108), kind=kOutput, calls=%fused_computation.1.clone.1 | convolution fusion | flops 610271744 | bytes 31457344 | tf_op jit(solution)/shard_map/while/body/eval_jaxpr/dot_general | solution.py:110
  444.3 4.5 copy-done
  449.2 7.9 %convert_element_type.64 = bf16[32,98304]{1,0:T(8,128)(2,1)} convert(f32[32,98304]{1,0:T(8,128)} %get-tuple-element.68) | non-fusion elementwise | flops 3145728 | bytes 18874368 | tf_op jit(solution)/shard_map/convert_element_type | solution.py:129
  457.1 7.8 %convert_element_type.65 = bf16[32,98304]{1,0:T(8,128)(2,1)} convert(f32[32,98304]{1,0:T(8,128)} %get-tuple-element.69) | non-fusion elementwise | flops 3145728 | bytes 18874368 | tf_op jit(solution)/shard_map/convert_element_type | solution.py:132
  466.9 24.9 %all-reduce = bf16[32,128]{1,0:T(8,128)(2,1)S(1)} all-reduce(bf16[32,128]{1,0:T(8,128)(2,1)S(1)} %convert_element_type.63), channel_id=2, replica_groups=mesh['dp'=16,'comp'=16] {'dp'}, use_global_device_ids=true, to_apply=%region_7.8.clone | all-reduce | flops 4096 | bytes 16384
  493.0 131.2 %all-reduce.6.cloned.1.call-done = (bf16[32,98304]{1,0:T(8,128)(2,1)}, bf16[32,98304]{1,0:T(8,128)(2,1)}) async-done(((bf16[32,98304]{1,0:T(8,128)(2,1)}, bf16[32,98304]{1,0:T(8,128)(2,1)}), (bf16[32,98304]{1,0:T(8,128)(2,1)}, bf16[32,98304]{1,0:T(8,128)(2,1)})) %all-reduce.6.cloned.1.call-update) | async-done | bytes 12582928
  624.2 2.5 dynamic-slice_convert_fusion
  626.7 1.6 reshape.129
  628.3 1.6 reshape.131
  (114 shorter events, 10.0 us)
Async XLA Ops:
  11.5 9.6 %copy-start.2 = (bf16[256]{0:T(256)(128)(2,1)S(1)}, bf16[256]{0:T(256)(128)(2,1)}, u32[]{:S(2)}) copy-start(bf16[256]{0:T(256)(128)(2,1)} %param.11) | copy-start | bytes 1540
  11.5 187.7 %copy-start.1 = (s32[16,4]{0,1:T(4,128)S(1)}, s32[16,4]{0,1:T(4,128)}, u32[]{:S(2)}) copy-start(s32[16,4]{0,1:T(4,128)} %param.8) | copy-start | bytes 772
  11.5 187.8 %all-to-all-start = ((bf16[16,256,768]{2,1,0:T(8,128)(2,1)}), bf16[16,256,768]{2,1,0:T(8,128)(2,1)}, u32[]{:S(2)}, u32[]{:S(2)}) async-start(bf16[16,256,768]{2,1,0:T(8,128)(2,1)} %stack.2), calls=%async_computation | async-start | bytes 12582912 | tf_op jit(solution)/shard_map/all_to_all | solution.py:70
  20.3 183.8 %all-gather.3.cloned.1.call-start = ((), (), s32[]{:S(2)}) async-start(), calls=%async_computation.1 | async-start | bytes 6684672 | tf_op jit(solution)/shard_map/all_gather | solution.py:76
  21.0 603.2 %all-reduce.6.cloned.1.call-start = ((), (), s32[]{:S(2)}) async-start(), calls=%async_computation.2 | async-start | bytes 25165824
  245.6 7.0 %slice-start.3 = ((s8[6291456]{0:T(1024)(128)(4,1)}), s8[4194304]{0:T(1024)(128)(4,1)S(1)}, s32[]{:S(2)}) async-start(s8[6291456]{0:T(1024)(128)(4,1)} %bitcast.138), calls=%async_computation.6 | async-start | bytes 8388608 | tf_op jit(solution)/shard_map/while
  249.6 3.1 slice-start.4
  265.4 16.6 %slice-start = ((s8[12582912]{0:T(1024)(128)(4,1)}), s8[4194304]{0:T(1024)(128)(4,1)S(1)}, s32[]{:S(2)}) async-start(s8[12582912]{0:T(1024)(128)(4,1)} %bitcast.134), calls=%async_computation.3 | async-start | bytes 8388608 | tf_op jit(solution)/shard_map/while
  265.4 16.6 %slice-start.1 = ((s8[12582912]{0:T(1024)(128)(4,1)}), s8[4194304]{0:T(1024)(128)(4,1)S(1)}, s32[]{:S(2)}) async-start(s8[12582912]{0:T(1024)(128)(4,1)} %bitcast.134), calls=%async_computation.4 | async-start | bytes 8388608 | tf_op jit(solution)/shard_map/while
  276.1 5.9 slice-start.2
  290.2 4.5 copy-start
  295.1 7.0 %slice-start.3 = ((s8[6291456]{0:T(1024)(128)(4,1)}), s8[4194304]{0:T(1024)(128)(4,1)S(1)}, s32[]{:S(2)}) async-start(s8[6291456]{0:T(1024)(128)(4,1)} %bitcast.138), calls=%async_computation.6 | async-start | bytes 8388608 | tf_op jit(solution)/shard_map/while
  299.1 3.1 slice-start.4
  314.9 18.4 %slice-start = ((s8[12582912]{0:T(1024)(128)(4,1)}), s8[4194304]{0:T(1024)(128)(4,1)S(1)}, s32[]{:S(2)}) async-start(s8[12582912]{0:T(1024)(128)(4,1)} %bitcast.134), calls=%async_computation.3 | async-start | bytes 8388608 | tf_op jit(solution)/shard_map/while
  314.9 18.4 %slice-start.1 = ((s8[12582912]{0:T(1024)(128)(4,1)}), s8[4194304]{0:T(1024)(128)(4,1)S(1)}, s32[]{:S(2)}) async-start(s8[12582912]{0:T(1024)(128)(4,1)} %bitcast.134), calls=%async_computation.4 | async-start | bytes 8388608 | tf_op jit(solution)/shard_map/while
  327.4 5.9 slice-start.2
  341.6 4.5 copy-start
  346.4 7.0 %slice-start.3 = ((s8[6291456]{0:T(1024)(128)(4,1)}), s8[4194304]{0:T(1024)(128)(4,1)S(1)}, s32[]{:S(2)}) async-start(s8[6291456]{0:T(1024)(128)(4,1)} %bitcast.138), calls=%async_computation.6 | async-start | bytes 8388608 | tf_op jit(solution)/shard_map/while
  350.4 3.1 slice-start.4
  366.3 18.4 %slice-start = ((s8[12582912]{0:T(1024)(128)(4,1)}), s8[4194304]{0:T(1024)(128)(4,1)S(1)}, s32[]{:S(2)}) async-start(s8[12582912]{0:T(1024)(128)(4,1)} %bitcast.134), calls=%async_computation.3 | async-start | bytes 8388608 | tf_op jit(solution)/shard_map/while
  366.3 18.4 %slice-start.1 = ((s8[12582912]{0:T(1024)(128)(4,1)}), s8[4194304]{0:T(1024)(128)(4,1)S(1)}, s32[]{:S(2)}) async-start(s8[12582912]{0:T(1024)(128)(4,1)} %bitcast.134), calls=%async_computation.4 | async-start | bytes 8388608 | tf_op jit(solution)/shard_map/while
  378.8 5.9 slice-start.2
  392.9 4.5 copy-start
  397.8 7.0 %slice-start.3 = ((s8[6291456]{0:T(1024)(128)(4,1)}), s8[4194304]{0:T(1024)(128)(4,1)S(1)}, s32[]{:S(2)}) async-start(s8[6291456]{0:T(1024)(128)(4,1)} %bitcast.138), calls=%async_computation.6 | async-start | bytes 8388608 | tf_op jit(solution)/shard_map/while
  401.8 3.1 slice-start.4
  417.6 18.4 %slice-start = ((s8[12582912]{0:T(1024)(128)(4,1)}), s8[4194304]{0:T(1024)(128)(4,1)S(1)}, s32[]{:S(2)}) async-start(s8[12582912]{0:T(1024)(128)(4,1)} %bitcast.134), calls=%async_computation.3 | async-start | bytes 8388608 | tf_op jit(solution)/shard_map/while
  417.6 18.4 %slice-start.1 = ((s8[12582912]{0:T(1024)(128)(4,1)}), s8[4194304]{0:T(1024)(128)(4,1)S(1)}, s32[]{:S(2)}) async-start(s8[12582912]{0:T(1024)(128)(4,1)} %bitcast.134), calls=%async_computation.4 | async-start | bytes 8388608 | tf_op jit(solution)/shard_map/while
  430.1 5.9 slice-start.2
  444.3 4.5 copy-start
  465.0 0.7 copy-start.3
Sparse Core Ops, SparseCore 0:
  22.9 133.8 all-gather.2
  465.1 159.0 all-reduce.5
